TPU v7x, 512 devices: a whole 4x8x8 slice. The times are simulated.
512 devices in a mesh: grp: 32 (over y, x), mlp: 16 (over z, core).
Axes of the slice: x: 4, y: 8, z: 8, core: 2. Of those that a mesh axis runs over, the one named last changes fastest.
Arguments:
- queries: bfloat16 [32, 128, 4096], P('grp'), may hold values from -70 to 70
- fresh_kv: bfloat16 [32, 128, 1024], P('grp', 'mlp'), may hold values from -5 to 5
- kv_pages: bfloat16 [32, 32, 128, 1024], P('grp', 'mlp'), may hold values from -5 to 5
- residual: bfloat16 [32, 128, 4096], P('grp'), may hold values from -3 to 3
- norm_gain: float32 [4096], replicated, may hold values from 0.5 to 1.5
- out_weight: bfloat16 [4096, 4096], P('mlp', 'grp'), may hold values from -0.09375 to 0.09375
- gate_weight: bfloat16 [4096, 6144], P('grp', 'mlp'), may hold values from -0.09375 to 0.09375
- up_weight: bfloat16 [4096, 6144], P('grp', 'mlp'), may hold values from -0.09375 to 0.09375
- down_weight: bfloat16 [6144, 4096], P('mlp', 'grp'), may hold values from -0.078125 to 0.078125
- page_table: int32 [32, 16, 12], P('grp'), may hold values from -1 to 31, as said below
- shared_pages: int32 [32, 4], P('grp'), may hold values from 0 to 31, as said below
- cache_lens: int32 [32, 16], P('grp'), may hold values from 513 to 2048, as said below
- prefill_offsets: int32 [32], P('grp'), may hold values from 1 to 512
Outputs:
- layer_out: bfloat16 [32, 128, 4096], P('grp', 'mlp')
Inputs may be any that keep to these rules, and one draw needn't show every extreme that they name: `page_table`: row d lists the pool pages that hold decode d's tokens after the shared prompt, in order, and -1 after its last page; no page appears twice in a group, and none is also a shared page. `shared_pages`: the pool pages of the group's shared prompt in order; they are the first 4 pages of every request of the group. `cache_lens`: decode d's cached tokens fill exactly its listed pages after the 4 shared pages; in every group one decode has the most.
All inputs are finite; a program needn't handle non-finite values.
Results may differ from a plain program's by a relative error of at most 0.029.
Values may be sent and summed in bfloat16 or wider, within the bound.
No kernel may reach another device: no remote copies, remote signals or barrier semaphores. Data moves between devices by JAX's collectives and lax.ppermute only.
A program may use at most 128 MiB of HBM per device.

v0:
```python
import jax
import jax.numpy as jnp
from jax import lax
from jax.sharding import PartitionSpec as P

HEADS = 32
KV_HEADS = 4
HEAD = 128
PAGE = 128
SHARED_PAGES = 4
PRIVATE_PAGES = 12
DECODES = 16
PREFILL = 112
ROWS = 128
NEG_FILL = -1e30
EPSILON = 1e-05


def merged(shard, axis, combine):
    everything = jax.tree.map(lambda part: lax.all_gather(part, axis), shard)
    leading = jax.tree.map(lambda part: part[0], everything)

    def step(k, so_far):
        return combine(so_far, jax.tree.map(lambda part: part[k], everything))

    return lax.fori_loop(1, lax.axis_size(axis), step, leading)


def page_layout(page_ids, table_group, shared_group):
    shared_match = shared_group[None, :] == page_ids[:, None]
    is_shared = jnp.any(shared_match, axis=1)
    shared_slot = jnp.sum(
        jnp.where(shared_match, jnp.arange(SHARED_PAGES, dtype=jnp.int32)[None, :], 0),
        axis=1,
        dtype=jnp.int32,
    )
    own_match = table_group[None, :, :] == page_ids[:, None, None]
    owner_id = (
        jnp.sum(
            jnp.where(own_match, jnp.arange(DECODES, dtype=jnp.int32)[None, :, None] + 1, 0),
            axis=(1, 2),
            dtype=jnp.int32,
        )
        - 1
    )
    own_slot = jnp.sum(
        jnp.where(own_match, jnp.arange(PRIVATE_PAGES, dtype=jnp.int32)[None, None, :], 0),
        axis=(1, 2),
        dtype=jnp.int32,
    )
    page_base = jnp.where(is_shared, shared_slot * PAGE, (SHARED_PAGES + own_slot) * PAGE)
    key_pos = (page_base[:, None] + jnp.arange(PAGE, dtype=jnp.int32)[None, :]).reshape(-1)
    key_shared = jnp.repeat(is_shared, PAGE)
    key_owner = jnp.repeat(jnp.where(is_shared, -1, owner_id), PAGE)
    return (key_pos, key_shared, key_owner)


def row_layout(lens_group, offset_value):
    row_ids = jnp.arange(ROWS, dtype=jnp.int32)
    is_prefill = row_ids < PREFILL
    decode_id = jnp.where(is_prefill, -2, row_ids - PREFILL)
    picked = decode_id[:, None] == jnp.arange(DECODES, dtype=jnp.int32)[None, :]
    decode_limit = jnp.sum(jnp.where(picked, lens_group[None, :], 0), axis=1, dtype=jnp.int32)
    limit = jnp.where(is_prefill, offset_value, decode_limit)
    return (row_ids, is_prefill, decode_id, limit)


def cache_visible(key_pos, key_shared, key_owner, decode_id, limit):
    belongs = key_shared[None, :] | (key_owner[None, :] == decode_id[:, None])
    return belongs & (key_pos[None, :] < limit[:, None])


def fresh_visible(key_rows, row_ids, is_prefill):
    before = (key_rows[None, :] < PREFILL) & (key_rows[None, :] <= row_ids[:, None])
    return jnp.where(is_prefill[:, None], before, key_rows[None, :] == row_ids[:, None])


def rms_norm(values, norm_gain):
    return (
        values * lax.rsqrt(jnp.mean(values * values, axis=1, keepdims=True) + EPSILON) * norm_gain
    ).astype(jnp.bfloat16)


def combine_parts(earlier_part, later_part):
    peak_one, total_one, mixed_one = earlier_part
    peak_two, total_two, mixed_two = later_part
    row_peak = jnp.maximum(peak_one, peak_two)
    factor_one = jnp.exp(peak_one - row_peak)
    factor_two = jnp.exp(peak_two - row_peak)
    row_total = total_one * factor_one + total_two * factor_two
    row_number, head_number = row_peak.shape
    weighted = (
        mixed_one.reshape(row_number, head_number, -1) * factor_one[:, :, None]
        + mixed_two.reshape(row_number, head_number, -1) * factor_two[:, :, None]
    )
    return (row_peak, row_total, weighted.reshape(row_number, -1))


def local(
    queries,
    fresh_kv,
    kv_pages,
    residual,
    norm_gain,
    out_weight,
    gate_weight,
    up_weight,
    down_weight,
    page_table,
    shared_pages,
    cache_lens,
    prefill_offsets,
):
    out_rows, gate_cols, up_cols, down_rows = (
        lax.all_gather(out_weight, "grp", axis=1, tiled=True),
        lax.all_gather(gate_weight, "grp", axis=0, tiled=True),
        lax.all_gather(up_weight, "grp", axis=0, tiled=True),
        lax.all_gather(down_weight, "grp", axis=1, tiled=True),
    )
    mlp_index = lax.axis_index("mlp")
    pool_pages = kv_pages.shape[1]
    own_count = fresh_kv.shape[1]
    page_ids = mlp_index * pool_pages + jnp.arange(pool_pages, dtype=jnp.int32)
    key_rows = mlp_index * own_count + jnp.arange(own_count, dtype=jnp.int32)
    key_pos, key_shared, key_owner = page_layout(page_ids, page_table[0], shared_pages[0])
    row_ids, is_prefill, decode_id, limit = row_layout(cache_lens[0], prefill_offsets[0])
    cache_seen = cache_visible(key_pos, key_shared, key_owner, decode_id, limit)
    fresh_seen = fresh_visible(key_rows, row_ids, is_prefill)
    cached = kv_pages[0].reshape(pool_pages * PAGE, 2, KV_HEADS, HEAD)
    fresh = fresh_kv[0].reshape(own_count, 2, KV_HEADS, HEAD)
    grouped = HEADS // KV_HEADS
    query_heads = queries[0].reshape(ROWS, KV_HEADS, grouped, HEAD)
    score_scale = HEAD ** (-0.5)
    peak_list = []
    total_list = []
    mixed_list = []
    for head_index in range(KV_HEADS):
        query_block = query_heads[:, head_index]
        cache_scores = (
            jnp.einsum(
                "rgh,kh->rgk",
                query_block,
                cached[:, 0, head_index],
                preferred_element_type=jnp.float32,
            )
            * score_scale
        )
        fresh_scores = (
            jnp.einsum(
                "rgh,kh->rgk",
                query_block,
                fresh[:, 0, head_index],
                preferred_element_type=jnp.float32,
            )
            * score_scale
        )
        cache_scores = jnp.where(cache_seen[:, None, :], cache_scores, NEG_FILL)
        fresh_scores = jnp.where(fresh_seen[:, None, :], fresh_scores, NEG_FILL)
        row_peak = jnp.maximum(jnp.max(cache_scores, axis=2), jnp.max(fresh_scores, axis=2))
        cache_exps = jnp.where(
            cache_seen[:, None, :], jnp.exp(cache_scores - row_peak[:, :, None]), 0.0
        )
        fresh_exps = jnp.where(
            fresh_seen[:, None, :], jnp.exp(fresh_scores - row_peak[:, :, None]), 0.0
        )
        row_total = jnp.sum(cache_exps, axis=2) + jnp.sum(fresh_exps, axis=2)
        weighted = jnp.einsum(
            "rgk,kh->rgh",
            cache_exps.astype(jnp.bfloat16),
            cached[:, 1, head_index],
            preferred_element_type=jnp.float32,
        )
        weighted = weighted + jnp.einsum(
            "rgk,kh->rgh",
            fresh_exps.astype(jnp.bfloat16),
            fresh[:, 1, head_index],
            preferred_element_type=jnp.float32,
        )
        peak_list.append(row_peak)
        total_list.append(row_total)
        mixed_list.append(weighted)
    row_peak = jnp.stack(peak_list, axis=1).reshape(ROWS, HEADS)
    row_total = jnp.stack(total_list, axis=1).reshape(ROWS, HEADS)
    weighted = jnp.stack(mixed_list, axis=1).reshape(ROWS, HEADS * HEAD)
    row_peak, row_total, weighted = merged((row_peak, row_total, weighted), "mlp", combine_parts)
    attended = (
        (weighted.reshape(ROWS, HEADS, HEAD) / row_total[:, :, None])
        .reshape(ROWS, HEADS * HEAD)
        .astype(jnp.bfloat16)
    )
    feature_count = out_rows.shape[0]
    own_features = lax.dynamic_slice_in_dim(attended, mlp_index * feature_count, feature_count, 1)
    row_begin = mlp_index * own_count
    projected = lax.psum(
        jnp.dot(own_features, out_rows, preferred_element_type=jnp.float32).astype(jnp.bfloat16),
        "mlp",
    ).astype(jnp.float32)
    updated = residual[0].astype(jnp.float32) + projected
    normed = rms_norm(updated, norm_gain)
    carried_rows = lax.dynamic_slice_in_dim(updated, row_begin, own_count, 0)
    gate_act = jnp.dot(normed, gate_cols, preferred_element_type=jnp.float32)
    up_act = jnp.dot(normed, up_cols, preferred_element_type=jnp.float32)
    hidden = (jax.nn.silu(gate_act) * up_act).astype(jnp.bfloat16)
    returned = lax.psum_scatter(
        jnp.dot(hidden, down_rows, preferred_element_type=jnp.float32).astype(jnp.bfloat16),
        "mlp",
        scatter_dimension=0,
        tiled=True,
    ).astype(jnp.float32)
    return (carried_rows + returned).astype(jnp.bfloat16)[None]


def solution(mesh):
    placed = (
        P("grp", None, None),
        P("grp", "mlp", None),
        P("grp", "mlp", None, None),
        P("grp", None, None),
        P(),
        P("mlp", "grp"),
        P("grp", "mlp"),
        P("grp", "mlp"),
        P("mlp", "grp"),
        P("grp", None, None),
        P("grp", None),
        P("grp", None),
        P("grp"),
    )
    return jax.shard_map(
        local, mesh=mesh, in_specs=placed, out_specs=P("grp", "mlp", None), check_vma=False
    )
```

profile of v0, /device:TPU:2, one launch (start us, length us, event | category | flops | bytes accessed | tf_op | source)
XLA Modules:
  0.0 786.7 jit_solution(5587190281900795073)
XLA Ops:
  21.2 2.0 fusion.102
  24.1 2.9 fusion.100
  37.2 2.4 fusion.17
  39.7 24.5 %all_gather.22 = f32[16,128,32]{1,2,0:T(8,128)S(1)} all-gather(f32[1,128,32]{1,2,0:T(8,128)S(1)} %maximum_bitcast_fusion.1), channel_id=1, replica_groups=mesh['grp'=32,'mlp'=16] {'mlp'}, dimensions={0}, use_global_device_ids=true | all-gather | bytes 278528 | tf_op jit(solution)/shard_map/all_gather | solution.py:20
  64.3 16.6 %all_gather.21 = f32[16,128,32]{1,2,0:T(8,128)S(1)} all-gather(f32[1,128,32]{1,2,0:T(8,128)S(1)} %maximum_bitcast_fusion), channel_id=1, replica_groups=mesh['grp'=32,'mlp'=16] {'mlp'}, dimensions={0}, use_global_device_ids=true | all-gather | bytes 278528 | tf_op jit(solution)/shard_map/all_gather | solution.py:20
  81.0 139.0 %all-gather.6.cloned.1.call-done = f32[16,128,4096]{2,1,0:T(8,128)} async-done(((f32[1,128,4096]{2,1,0:T(8,128)}), f32[16,128,4096]{2,1,0:T(8,128)}) %all-gather.6.cloned.1.call-update) | async-done | bytes 33554448 | tf_op jit(solution)/shard_map/all_gather | solution.py:20
  221.8 108.8 %while.19 = (s32[]{:T(128)}, f32[128,32]{1,0:T(8,128)S(1)}, f32[128,32]{1,0:T(8,128)S(1)}, f32[128,4096]{1,0:T(8,128)S(1)}, f32[16,128,32]{1,2,0:T(8,128)S(1)}, ...) while((s32[]{:T(128)}, f32[128,32]{1,0:T(8,128)S(1)}, ...), condition=%wide.region_22.23_spmd, body=%wide.region_21.22_spmd.sunk | while | flops 1597445 | bytes 14975127 | solution.py:26
  223.3 5.7 fusion.115
  230.6 5.7 fusion.115
  237.8 5.7 fusion.115
  245.1 5.7 fusion.115
  252.3 5.7 fusion.115
  259.6 5.7 fusion.115
  266.8 5.7 fusion.115
  274.1 5.7 fusion.115
  281.3 5.7 fusion.115
  288.6 5.7 fusion.115
  295.9 5.7 fusion.115
  303.1 5.7 fusion.115
  310.4 5.7 fusion.115
  317.6 5.7 fusion.115
  324.9 5.7 fusion.115
  331.2 3.0 copy.115
  334.2 3.2 convolution_convert_fusion.1
  339.2 114.0 %all-reduce.2.cloned.1.call-done = bf16[128,4096]{1,0:T(8,128)(2,1)} async-done(((bf16[128,4096]{1,0:T(8,128)(2,1)}), bf16[128,4096]{1,0:T(8,128)(2,1)}) %all-reduce.2.cloned.1.call-update) | async-done | bytes 1048592 | tf_op jit(solution)/shard_map/psum | solution.py:194
  453.3 3.0 convert_add_fusion
  456.2 84.0 %all-gather.10.cloned.1.call-done = bf16[4096,384]{1,0:T(8,128)(2,1)} async-done(((bf16[128,384]{1,0:T(8,128)(2,1)}), bf16[4096,384]{1,0:T(8,128)(2,1)}) %all-gather.10.cloned.1.call-update) | async-done | bytes 3145744 | tf_op jit(solution)/shard_map/all_gather | solution.py:116
  540.3 2.6 fusion.97
  542.9 83.0 %all-gather.12.cloned.1.call-done = bf16[4096,384]{1,0:T(8,128)(2,1)} async-done(((bf16[128,384]{1,0:T(8,128)(2,1)}), bf16[4096,384]{1,0:T(8,128)(2,1)}) %all-gather.12.cloned.1.call-update) | async-done | bytes 3145744 | tf_op jit(solution)/shard_map/all_gather | solution.py:117
  625.9 86.5 %all-gather.14.cloned.1.call-done = bf16[384,4096]{1,0:T(8,128)(2,1)} async-done(((bf16[384,128]{1,0:T(8,128)(2,1)}), bf16[384,4096]{1,0:T(8,128)(2,1)}) %all-gather.14.cloned.1.call-update) | async-done | bytes 3145744 | tf_op jit(solution)/shard_map/all_gather | solution.py:118
  712.5 5.3 convolution_convert_fusion
  717.8 60.5 %reduce-scatter.2.cloned.1.call-done = bf16[8,4096]{1,0:T(8,128)(2,1)} async-done(((bf16[128,4096]{1,0:T(8,128)(2,1)}), bf16[8,4096]{1,0:T(8,128)(2,1)}) %reduce-scatter.2.cloned.1.call-update) | async-done | bytes 65552 | tf_op jit(solution)/shard_map/reduce_scatter | solution.py:204
  (206 shorter events, 52.8 us)
Async XLA Ops:
  6.5 3.5 copy-start.16
  6.5 6.6 copy-start.15
  6.5 7.4 copy-start.8
  6.5 213.5 %all-gather.6.cloned.1.call-start = ((), (), s32[]{:S(2)}) async-start(), calls=%async_computation.1 | async-start | bytes 35651584 | tf_op jit(solution)/shard_map/all_gather | solution.py:20
  10.0 7.5 copy-start.7
  11.7 4.6 copy-start.20
  19.4 9.8 %copy-start.2 = (f32[128,8,256]{2,0,1:T(8,128)}, f32[128,8,256]{2,0,1:T(8,128)S(1)}, u32[]{:S(2)}) copy-start(f32[128,8,256]{2,0,1:T(8,128)S(1)} %get-tuple-element.256) | copy-start | bytes 3145732
  23.2 7.6 copy-start.4
  24.1 5.2 copy-start.10
  27.1 2.1 copy-start.19
  27.8 1.9 copy-start.11
  28.2 2.5 copy-start.18
  28.2 2.6 copy-start.9
  29.3 1.9 copy-start.12
  29.7 2.5 copy-start.17
  29.7 2.5 copy-start.6
  30.8 1.8 copy-start.13
  35.6 1.2 copy-start.3
  35.6 1.5 copy-start.5
  35.7 298.6 %all-gather.8.cloned.1.call-start = ((), (), s32[]{:S(2)}) async-start(), calls=%async_computation.2 | async-start | bytes 2162688 | tf_op jit(solution)/shard_map/all_gather | solution.py:115
  36.4 416.8 %all-reduce.2.cloned.1.call-start = ((), (), s32[]{:S(2)}) async-start(), calls=%async_computation.3 | async-start | bytes 2097152 | tf_op jit(solution)/shard_map/psum | solution.py:194
  334.2 119.0 %copy-start = (bf16[1,128,4096]{2,1,0:T(8,128)(2,1)S(1)}, bf16[1,128,4096]{2,1,0:T(8,128)(2,1)}, u32[]{:S(2)}) copy-start(bf16[1,128,4096]{2,1,0:T(8,128)(2,1)} %param.18) | copy-start | bytes 3145732
  337.4 202.8 %all-gather.10.cloned.1.call-start = ((), (), s32[]{:S(2)}) async-start(), calls=%async_computation.4 | async-start | bytes 3244032 | tf_op jit(solution)/shard_map/all_gather | solution.py:116
  338.0 287.9 %all-gather.12.cloned.1.call-start = ((), (), s32[]{:S(2)}) async-start(), calls=%async_computation.5 | async-start | bytes 3244032 | tf_op jit(solution)/shard_map/all_gather | solution.py:117
  338.6 373.9 %all-gather.14.cloned.1.call-start = ((), (), s32[]{:S(2)}) async-start(), calls=%async_computation.6 | async-start | bytes 3244032 | tf_op jit(solution)/shard_map/all_gather | solution.py:118
  339.2 201.1 %copy-start.14 = (f32[4096]{0:T(1024)S(1)}, f32[4096]{0:T(1024)}, u32[]{:S(2)}) copy-start(f32[4096]{0:T(1024)} %param.19) | copy-start | bytes 49156
  339.2 439.1 %reduce-scatter.2.cloned.1.call-start = ((), (), s32[]{:S(2)}) async-start(), calls=%async_computation.7 | async-start | bytes 1114112 | tf_op jit(solution)/shard_map/reduce_scatter | solution.py:204
  453.2 87.0 %copy-start.1 = (bf16[128,4096]{1,0:T(8,128)(2,1)S(1)}, bf16[128,4096]{1,0:T(8,128)(2,1)}, u32[]{:S(2)}) copy-start(bf16[128,4096]{1,0:T(8,128)(2,1)} %all-reduce.2.cloned.1.call-done) | copy-start | bytes 3145732
Sparse Core Ops, SparseCore 0:
  35.8 184.2 all-gather.5
  223.1 77.9 all-gather.7
  337.5 115.6 all-reduce.1
  456.7 83.4 all-gather.9
  543.8 82.1 all-gather.11
  629.3 83.1 all-gather.13
  717.9 60.2 reduce-scatter.1
where the time goes:
time: 788 us; the launch traced here: 787 us
  waiting for transfers between devices  569 us (72%)
  other arithmetic  97.4 us (12%)
  blocking collectives  41.1 us (5%)
  local copies, waits for them, and re-layouts  35.7 us (5%)
  matrix products  27.6 us (4%)
  between operations  14.6 us (2%)
    all_gather x1, waiting for transfers between devices, merged(): everything = jax.tree.map(lambda part: lax.all_gather(part, axis), shard)  139 us
    psum x1, waiting for transfers between devices, local(): lax.psum(jnp.dot(own_features, out_rows, preferred_element_type=jnp.float...  114 us
    all_gather x1, waiting for transfers between devices, local(): lax.all_gather(down_weight, 'grp', axis=1, tiled=True)  86.5 us
    add x15, other arithmetic, combine_parts(): mixed_one.reshape(row_number, head_number, -1) * factor_one[:, :, None]  86.1 us
    all_gather x1, waiting for transfers between devices, local(): lax.all_gather(gate_weight, 'grp', axis=0, tiled=True)  84 us
    all_gather x1, waiting for transfers between devices, local(): lax.all_gather(up_weight, 'grp', axis=0, tiled=True)  83 us
    reduce_scatter x1, waiting for transfers between devices, local(): lax.psum_scatter(jnp.dot(hidden, down_rows, preferred_element_type=jnp.fl...  60.5 us
    all_gather x2, blocking collectives, merged(): everything = jax.tree.map(lambda part: lax.all_gather(part, axis), shard)  41.1 us
  transfers between devices with their start and end apart: 7, of which 6 were waited for; matrix products, arithmetic and copies ran while one was open for 15% of the time, Pallas kernels for 0%

commit v1 on v0

--- a/solution.py
+++ b/solution.py
@@ -1,3 +1,4 @@
+import functools
 import jax
 import jax.numpy as jnp
 from jax import lax
@@ -14,6 +15,19 @@
 ROWS = 128
 NEG_FILL = -1e30
 EPSILON = 1e-05
+
+
+def turn_skins_by_axis(inner_x, comm_axis):
+    rows = []
+    shares = jax.lax.axis_size(comm_axis)
+    for at in range(inner_x.ndim):
+        rows.append(shares if at == 1 else 1)
+    return jax.lax.all_to_all(
+        jnp.tile(inner_x, rows), comm_axis, split_axis=1, concat_axis=1, tiled=True
+    )
+
+
+produce_stocks = functools.partial(turn_skins_by_axis, comm_axis="grp")
 
 
 def merged(shard, axis, combine):
@@ -115,7 +129,7 @@
         lax.all_gather(out_weight, "grp", axis=1, tiled=True),
         lax.all_gather(gate_weight, "grp", axis=0, tiled=True),
         lax.all_gather(up_weight, "grp", axis=0, tiled=True),
-        lax.all_gather(down_weight, "grp", axis=1, tiled=True),
+        produce_stocks(down_weight),
     )
     mlp_index = lax.axis_index("mlp")
     pool_pages = kv_pages.shape[1]

time: 788 us -> 702 us (0.89)
  waiting for transfers between devices: 569 us -> 467 us
  starting transfers between devices: 0.24 us -> 10.3 us
    all_gather x1 -> x0, waiting for transfers between devices: 86.5 us -> none  [local(): lax.all_gather(down_weight, 'grp', axis=1, tiled=True)]
    psum x1, waiting for transfers between devices: 114 us -> 29.6 us  [local(): lax.psum(jnp.dot(own_features, out_rows, preferred_element_type=jnp.float...]
    all_to_all x0 -> x1, waiting for transfers between devices: none -> 71.1 us  [turn_skins_by_axis(): jax.lax.all_to_all(jnp.tile(inner_x, rows), comm_axis, split_axis=1, conc...]
    all_to_all x0 -> x1, starting transfers between devices: none -> 9.88 us  [turn_skins_by_axis(): jax.lax.all_to_all(jnp.tile(inner_x, rows), comm_axis, split_axis=1, conc...]
  transfers between devices with their start and end apart: 7 -> 7, of which waited for: 6 -> 6; matrix products, arithmetic and copies ran while one was open for 15% -> 18% of each run, Pallas kernels for 0% -> 0%
where the time goes in v1:
time: 702 us; the launch traced here: 700 us
  waiting for transfers between devices  467 us (67%)
  other arithmetic  97.6 us (14%)
  blocking collectives  41.2 us (6%)
  local copies, waits for them, and re-layouts  41 us (6%)
  matrix products  28.2 us (4%)
  between operations  14.6 us (2%)
  starting transfers between devices  10.3 us (1%)
    all_gather x1, waiting for transfers between devices, merged(): everything = jax.tree.map(lambda part: lax.all_gather(part, axis), shard)  139 us
    add x15, other arithmetic, combine_parts(): mixed_one.reshape(row_number, head_number, -1) * factor_one[:, :, None]  86.1 us
    all_gather x1, waiting for transfers between devices, local(): lax.all_gather(gate_weight, 'grp', axis=0, tiled=True)  83.9 us
    all_gather x1, waiting for transfers between devices, local(): lax.all_gather(up_weight, 'grp', axis=0, tiled=True)  82.4 us
    all_to_all x1, waiting for transfers between devices, turn_skins_by_axis(): jax.lax.all_to_all(jnp.tile(inner_x, rows), comm_axis, split_axis=1, conc...  71.1 us
    reduce_scatter x1, waiting for transfers between devices, local(): lax.psum_scatter(jnp.dot(hidden, down_rows, preferred_element_type=jnp.fl...  59.2 us
    all_gather x2, blocking collectives, merged(): everything = jax.tree.map(lambda part: lax.all_gather(part, axis), shard)  41.2 us
    psum x1, waiting for transfers between devices, local(): lax.psum(jnp.dot(own_features, out_rows, preferred_element_type=jnp.float...  29.6 us
  transfers between devices with their start and end apart: 7, of which 6 were waited for; matrix products, arithmetic and copies ran while one was open for 18% of the time, Pallas kernels for 0%

profile of v1, /device:TPU:2, one launch (start us, length us, event | category | flops | bytes accessed | tf_op | source)
XLA Modules:
  0.0 700.4 jit_solution(10766384011892757958)
XLA Ops:
  24.1 2.9 fusion.100
  39.7 24.5 %all_gather.19 = f32[16,128,32]{1,2,0:T(8,128)S(1)} all-gather(f32[1,128,32]{1,2,0:T(8,128)S(1)} %maximum_bitcast_fusion.1), channel_id=1, replica_groups=mesh['grp'=32,'mlp'=16] {'mlp'}, dimensions={0}, use_global_device_ids=true | all-gather | bytes 278528 | tf_op jit(solution)/shard_map/all_gather | solution.py:34
  64.3 16.6 %all_gather.18 = f32[16,128,32]{1,2,0:T(8,128)S(1)} all-gather(f32[1,128,32]{1,2,0:T(8,128)S(1)} %maximum_bitcast_fusion), channel_id=1, replica_groups=mesh['grp'=32,'mlp'=16] {'mlp'}, dimensions={0}, use_global_device_ids=true | all-gather | bytes 278528 | tf_op jit(solution)/shard_map/all_gather | solution.py:34
  81.0 139.0 %all-gather.5.cloned.1.call-done = f32[16,128,4096]{2,1,0:T(8,128)} async-done(((f32[1,128,4096]{2,1,0:T(8,128)}), f32[16,128,4096]{2,1,0:T(8,128)}) %all-gather.5.cloned.1.call-update) | async-done | bytes 33554448 | tf_op jit(solution)/shard_map/all_gather | solution.py:34
  221.8 108.8 %while.19 = (s32[]{:T(128)}, f32[128,32]{1,0:T(8,128)S(1)}, f32[128,32]{1,0:T(8,128)S(1)}, f32[128,4096]{1,0:T(8,128)S(1)}, f32[16,128,32]{1,2,0:T(8,128)S(1)}, ...) while((s32[]{:T(128)}, f32[128,32]{1,0:T(8,128)S(1)}, ...), condition=%wide.region_22.23_spmd, body=%wide.region_21.22_spmd.sunk | while | flops 1597445 | bytes 14975127 | solution.py:40
  223.3 5.7 fusion.115
  230.6 5.7 fusion.115
  237.8 5.7 fusion.115
  245.1 5.7 fusion.115
  252.3 5.7 fusion.115
  259.6 5.7 fusion.115
  266.8 5.7 fusion.115
  274.1 5.7 fusion.115
  281.3 5.7 fusion.115
  288.6 5.7 fusion.115
  295.9 5.7 fusion.115
  303.1 5.7 fusion.115
  310.4 5.7 fusion.115
  317.6 5.7 fusion.115
  324.9 5.7 fusion.115
  331.2 3.0 copy.136
  334.2 3.1 convolution_convert_fusion.1
  340.4 9.9 %all-to-all-start = ((bf16[384,32,128]{2,0,1:T(8,128)(2,1)}), bf16[384,32,128]{2,0,1:T(8,128)(2,1)S(1)}, u32[]{:S(2)}, u32[]{:S(2)}) async-start(bf16[384,32,128]{2,0,1:T(8,128)(2,1)} %tile.2), calls=%async_computation | async-start | bytes 6291456 | tf_op jit(solution)/shard_map/all_to_all | solution.py:25
  351.1 71.1 %all-to-all-done = bf16[384,32,128]{2,0,1:T(8,128)(2,1)S(1)} async-done(((bf16[384,32,128]{2,0,1:T(8,128)(2,1)}), bf16[384,32,128]{2,0,1:T(8,128)(2,1)S(1)}, u32[]{:S(2)}, u32[]{:S(2)}) %all-to-all-start) | async-done | bytes 3145760 | tf_op jit(solution)/shard_map/all_to_all | solution.py:25
  422.3 2.9 copy.97
  425.1 29.6 %all-reduce.2.cloned.1.call-done = bf16[128,4096]{1,0:T(8,128)(2,1)} async-done(((bf16[128,4096]{1,0:T(8,128)(2,1)}), bf16[128,4096]{1,0:T(8,128)(2,1)}) %all-reduce.2.cloned.1.call-update) | async-done | bytes 1048592 | tf_op jit(solution)/shard_map/psum | solution.py:208
  454.7 3.2 convert_add_fusion
  458.0 83.9 %all-gather.9.cloned.1.call-done = bf16[4096,384]{1,0:T(8,128)(2,1)} async-done(((bf16[128,384]{1,0:T(8,128)(2,1)}), bf16[4096,384]{1,0:T(8,128)(2,1)}) %all-gather.9.cloned.1.call-update) | async-done | bytes 3145744 | tf_op jit(solution)/shard_map/all_gather | solution.py:130
  541.8 3.3 fusion.97
  545.1 82.4 %all-gather.11.cloned.1.call-done = bf16[4096,384]{1,0:T(8,128)(2,1)} async-done(((bf16[128,384]{1,0:T(8,128)(2,1)}), bf16[4096,384]{1,0:T(8,128)(2,1)}) %all-gather.11.cloned.1.call-update) | async-done | bytes 3145744 | tf_op jit(solution)/shard_map/all_gather | solution.py:131
  627.5 5.3 convolution_convert_fusion
  632.8 59.2 %reduce-scatter.2.cloned.1.call-done = bf16[8,4096]{1,0:T(8,128)(2,1)} async-done(((bf16[128,4096]{1,0:T(8,128)(2,1)}), bf16[8,4096]{1,0:T(8,128)(2,1)}) %reduce-scatter.2.cloned.1.call-update) | async-done | bytes 65552 | tf_op jit(solution)/shard_map/reduce_scatter | solution.py:218
  (207 shorter events, 59.3 us)
Async XLA Ops:
  6.5 3.5 copy-start.16
  6.5 6.6 copy-start.15
  6.5 7.4 %copy-start.7 = (bf16[1,2,128,1024]{3,2,1,0:T(8,128)(2,1)S(1)}, bf16[1,2,128,1024]{3,2,1,0:T(8,128)(2,1)}, u32[]{:S(2)}) copy-start(bf16[1,2,128,1024]{3,2,1,0:T(8,128)(2,1)} %param.17) | copy-start | bytes 1572868
  6.5 213.5 %all-gather.5.cloned.1.call-start = ((), (), s32[]{:S(2)}) async-start(), calls=%async_computation.2 | async-start | bytes 35651584 | tf_op jit(solution)/shard_map/all_gather | solution.py:34
  10.0 7.5 %copy-start.6 = (bf16[1,128,4096]{1,2,0:T(8,128)(2,1)}, bf16[1,128,4096]{1,2,0:T(8,128)(2,1)S(1)}, u32[]{:S(2)}) copy-start(bf16[1,128,4096]{1,2,0:T(8,128)(2,1)S(1)} %copy.79) | copy-start | bytes 3145732
  11.7 4.6 copy-start.20
  19.4 9.8 %copy-start.1 = (f32[128,8,256]{2,0,1:T(8,128)}, f32[128,8,256]{2,0,1:T(8,128)S(1)}, u32[]{:S(2)}) copy-start(f32[128,8,256]{2,0,1:T(8,128)S(1)} %get-tuple-element.263) | copy-start | bytes 3145732
  23.2 7.6 %copy-start.3 = (f32[128,8,256]{2,0,1:T(8,128)}, f32[128,8,256]{2,0,1:T(8,128)S(1)}, u32[]{:S(2)}) copy-start(f32[128,8,256]{2,0,1:T(8,128)S(1)} %get-tuple-element.259) | copy-start | bytes 3145732
  24.1 5.2 copy-start.9
  27.1 2.1 copy-start.19
  27.8 1.9 copy-start.10
  28.2 2.5 copy-start.18
  28.2 2.6 copy-start.8
  29.3 1.9 copy-start.11
  29.7 2.5 copy-start.17
  29.7 2.5 copy-start.5
  30.8 1.8 copy-start.12
  35.6 1.2 copy-start.2
  35.6 1.5 copy-start.4
  35.7 298.6 %all-gather.7.cloned.1.call-start = ((), (), s32[]{:S(2)}) async-start(), calls=%async_computation.3 | async-start | bytes 2162688 | tf_op jit(solution)/shard_map/all_gather | solution.py:129
  36.4 418.3 %all-reduce.2.cloned.1.call-start = ((), (), s32[]{:S(2)}) async-start(), calls=%async_computation.4 | async-start | bytes 2097152 | tf_op jit(solution)/shard_map/psum | solution.py:208
  334.2 3.7 copy-start.13
  337.4 204.4 %all-gather.9.cloned.1.call-start = ((), (), s32[]{:S(2)}) async-start(), calls=%async_computation.5 | async-start | bytes 3244032 | tf_op jit(solution)/shard_map/all_gather | solution.py:130
  340.4 81.9 %all-to-all-start = ((bf16[384,32,128]{2,0,1:T(8,128)(2,1)}), bf16[384,32,128]{2,0,1:T(8,128)(2,1)S(1)}, u32[]{:S(2)}, u32[]{:S(2)}) async-start(bf16[384,32,128]{2,0,1:T(8,128)(2,1)} %tile.2), calls=%async_computation | async-start | bytes 6291456 | tf_op jit(solution)/shard_map/all_to_all | solution.py:25
  350.3 277.2 %all-gather.11.cloned.1.call-start = ((), (), s32[]{:S(2)}) async-start(), calls=%async_computation.6 | async-start | bytes 3244032 | tf_op jit(solution)/shard_map/all_gather | solution.py:131
  350.9 341.2 %reduce-scatter.2.cloned.1.call-start = ((), (), s32[]{:S(2)}) async-start(), calls=%async_computation.7 | async-start | bytes 1114112 | tf_op jit(solution)/shard_map/reduce_scatter | solution.py:218
  425.1 116.7 %copy-start.14 = (f32[4096]{0:T(1024)S(1)}, f32[4096]{0:T(1024)}, u32[]{:S(2)}) copy-start(f32[4096]{0:T(1024)} %param.19) | copy-start | bytes 49156
  458.0 169.5 %copy-start = (bf16[384,32,128]{0,2,1:T(8,128)(2,1)S(1)}, bf16[384,32,128]{0,2,1:T(8,128)(2,1)}, u32[]{:S(2)}) copy-start(bf16[384,32,128]{0,2,1:T(8,128)(2,1)} %copy.97) | copy-start | bytes 9437188
Sparse Core Ops, SparseCore 0:
  35.8 184.2 all-gather.4
  223.1 77.9 all-gather.6
  337.5 117.1 all-reduce.1
  458.2 83.5 all-gather.8
  545.3 82.1 all-gather.10
  632.9 59.0 reduce-scatter.1
